TPU v7x, 32 devices: a whole 2x2x4 slice. The times are simulated.
32 devices in a mesh: groups: 2 (over y), blk: 8 (over z, core), width: 2 (over x).
Axes of the slice: x: 2, y: 2, z: 4, core: 2. Of those that a mesh axis runs over, the one named last changes fastest.
Arguments:
- tokens: bfloat16 [448, 4096], P(('groups', 'blk'), 'width'), parts along dimension 0, may hold values from -6 to 6
- grad_hidden: bfloat16 [448, 28672], P('groups', 'blk'), parts along dimension 0, may hold values from -2 to 2
- codes: bfloat16 [2, 4096, 28672], P(None, 'width', 'blk'), may hold values from -8 to 7, as said below
- scales: float32 [2, 32, 28672], P(None, 'width', 'blk'), may hold values from 0.0015625 to 0.015625
- pattern: int32 [224, 32], P('blk', 'width'), may hold values from 0 to 1
Outputs:
- grad_tokens: bfloat16 [448, 4096], P(('groups', 'blk'), 'width'), parts along dimension 0
- grad_log_scales: float32 [2, 64, 28672], P(None, ('groups', 'width'), 'blk'), parts along dimension 1
There are 2 independent parts, one for each index of `groups`. A program takes and returns all parts, laid end to end along the dimension named above; an argument that names none is the same for every part. Nothing has to cross between parts.
Inputs may be any that keep to these rules, and one draw needn't show every extreme that they name: `codes`: every code is a whole number.
All inputs are finite; a program needn't handle non-finite values.
Results may differ from a plain program's by a relative error of at most 0.017.
Values may be sent and summed in bfloat16 or wider, within the bound.
A program may use at most 192 MiB of HBM per device.

v0:
```python
import jax
import jax.numpy as jnp
from jax import lax
from jax.sharding import PartitionSpec as P


def dequantize(codes, scales, pattern):
    rows_tile = scales.shape[1]
    block = codes.shape[1] // rows_tile
    cols = codes.shape[2]
    mask = jnp.repeat(pattern.T, block, axis=1).astype(jnp.float32)
    factor = scales * mask[None]
    values = codes.astype(jnp.float32).reshape(2, rows_tile, block, cols) * factor[:, :, None, :]
    weight = values.reshape(codes.shape).astype(jnp.bfloat16)
    return (jnp.concatenate((weight[0], weight[1]), axis=1), factor)


def back_gates(hidden, upstream):
    half = upstream.shape[1]
    gate = hidden[:, :half]
    up = hidden[:, half:]
    grad_in = upstream.astype(jnp.float32)
    sig = jax.nn.sigmoid(gate)
    grad_gate = grad_in * up * sig * (1.0 + gate * (1.0 - sig))
    grad_up = grad_in * gate * sig
    return jnp.concatenate((grad_gate, grad_up), axis=1).astype(jnp.bfloat16)


def on_device(tokens, grad_hidden, codes, scales, pattern):
    cols_tile, rows_tile = pattern.shape
    block = codes.shape[1] // rows_tile
    slice_f = codes.shape[2]
    gathered = lax.all_gather(tokens, "blk", axis=0, tiled=True)
    joined, factor = dequantize(codes, scales, pattern)
    hidden = lax.psum(
        jnp.dot(gathered, joined, preferred_element_type=jnp.float32).astype(jnp.bfloat16), "width"
    ).astype(jnp.float32)
    grads = back_gates(hidden, grad_hidden)
    grad_tokens = lax.psum_scatter(
        lax.dot_general(
            grads, joined, (((1,), (1,)), ((), ())), preferred_element_type=jnp.float32
        ).astype(jnp.bfloat16),
        "blk",
        scatter_dimension=0,
        tiled=True,
    )
    weight_grad = lax.dot_general(
        gathered, grads, (((0,), (0,)), ((), ())), preferred_element_type=jnp.float32
    )
    codes_joined = jnp.concatenate((codes[0], codes[1]), axis=1).astype(jnp.float32)
    summed = (weight_grad * codes_joined).reshape(rows_tile, block, 2 * slice_f).sum(axis=1)
    factor_joined = jnp.concatenate((factor[0], factor[1]), axis=1)
    return (grad_tokens, (summed * factor_joined).reshape(rows_tile, 2, slice_f).transpose(1, 0, 2))


def solution(mesh):
    return jax.shard_map(
        on_device,
        mesh=mesh,
        in_specs=(
            P(("groups", "blk"), "width"),
            P("groups", "blk"),
            P(None, "width", "blk"),
            P(None, "width", "blk"),
            P("blk", "width"),
        ),
        out_specs=(P(("groups", "blk"), "width"), P(None, ("groups", "width"), "blk")),
        check_vma=False,
    )
```

profile of v0, /device:TPU:0, one launch (start us, length us, event | category | flops | bytes accessed | tf_op | source)
XLA Modules:
  0.0 245.3 jit_solution(5949424410235880979)
XLA Ops:
  7.2 0.7 convert_bitcast_fusion
  8.2 1.5 copy_multiply_fusion
  9.8 20.5 %fusion.1 = bf16[2,2048,3584]{2,1,0:T(8,128)(2,1)} fusion(bf16[2,2048,3584]{2,1,0:T(8,128)(2,1)} %param.7, f32[2,16,3584]{2,1,0:T(8,128)S(1)} %copy.11), kind=kLoop, calls=%fused_computation.3 | loop fusion | flops 44040192 | bytes 59179008 | tf_op jit(solution)/shard_map/convert_element_type | solution.py:14
  30.3 21.6 %slice_bitcast_fusion.1 = (bf16[2048,3584]{1,0:T(8,128)(2,1)}, bf16[2048,3584]{1,0:T(8,128)(2,1)}) fusion(bf16[2,2048,3584]{2,1,0:T(8,128)(2,1)} %fusion.1), kind=kLoop, calls=%fused_computation.8 | loop fusion | bytes 58720256 | tf_op jit(solution)/shard_map/squeeze | solution.py:15
  51.9 18.3 %all-gather = bf16[8,28,2048]{2,1,0:T(8,128)(2,1)S(1)} all-gather(bf16[1,28,2048]{2,1,0:T(8,128)(2,1)S(1)} %bitcast.40), channel_id=1, replica_groups=mesh['groups'=2,'blk'=8,'width'=2] {'blk'}, dimensions={0}, use_global_device_ids=true | all-gather | bytes 1032192 | tf_op jit(solution)/shard_map/all_gather | solution.py:33
  70.2 0.2 reshape.26
  70.4 14.7 %fusion.5 = bf16[224,7168]{1,0:T(8,128)(2,1)} fusion(bf16[224,2048]{1,0:T(8,128)(2,1)S(1)} %reshape.26, bf16[2048,3584]{1,0:T(8,128)(2,1)} %get-tuple-element.9, bf16[2048,3584]{1,0:T(8,128)(2,1)} %get-tuple-element.8), kind=kOutput, calls=%fused_computation.12 | convolution fusion | flops 6636994560 | bytes 33488896 | tf_op jit(solution)/shard_map/dot_general | solution.py:36
  85.2 1.1 slice_bitcast_fusion.5
  86.2 0.6 dynamic-slice.4
  87.5 21.6 %slice_bitcast_fusion.3 = (bf16[2048,3584]{1,0:T(8,128)(2,1)}, bf16[2048,3584]{1,0:T(8,128)(2,1)}) fusion(bf16[2,2048,3584]{2,1,0:T(8,128)(2,1)} %param.7), kind=kLoop, calls=%fused_computation.10 | loop fusion | bytes 58720256 | tf_op jit(solution)/shard_map/squeeze | solution.py:50
  109.1 65.0 %all-reduce.4.cloned.1.call-done = bf16[224,7168]{1,0:T(8,128)(2,1)} async-done(((bf16[224,7168]{1,0:T(8,128)(2,1)}), bf16[224,7168]{1,0:T(8,128)(2,1)}) %all-reduce.4.cloned.1.call-update) | async-done | bytes 3211280 | tf_op jit(solution)/shard_map/psum | solution.py:35
  174.0 2.6 %convert_element_type.47 = f32[224,7168]{1,0:T(8,128)S(1)} convert(bf16[224,7168]{1,0:T(8,128)(2,1)} %all-reduce.4.cloned.1.call-done) | non-fusion elementwise | flops 1605632 | bytes 9633792 | tf_op jit(solution)/shard_map/convert_element_type | solution.py:37
  176.7 1.6 fusion.8
  178.2 1.1 copy-done.1
  179.4 14.2 %fusion.11 = bf16[224,2048]{1,0:T(8,128)(2,1)} fusion(bf16[2048,3584]{1,0:T(8,128)(2,1)} %get-tuple-element.9, bf16[2048,3584]{1,0:T(8,128)(2,1)} %get-tuple-element.8, bf16[224,3584]{1,0:T(8,128)(2,1)S(1)} %get-tuple-element.11, bf16[224,3584]{1,0:T(8,128)(2,1)S(1)} %get-tuple-element.10), kind=kOutput, calls=%fused_computation.22 | convolution fusion | flops 6642270208 | bytes 33488896 | tf_op jit(solution)/shard_map/dot_general | solution.py:40
  193.6 22.4 %fusion = bf16[32,2048]{1,0:T(8,128)(2,1)S(1)} fusion(bf16[224,2048]{1,0:T(8,128)(2,1)} %fusion.11), kind=kCustom, calls=%all-reduce-scatter | all-reduce-scatter fusion | flops 524289 | bytes 1049088
  216.0 0.7 slice.38
  216.7 1.9 collective-permute-start
  218.7 14.2 %bitcast_reduce_fusion = f32[16,7168]{1,0:T(8,128)} fusion(bf16[224,2048]{1,0:T(8,128)(2,1)S(1)} %copy-done.3, bf16[2048,3584]{1,0:T(8,128)(2,1)} %get-tuple-element.7, bf16[2048,3584]{1,0:T(8,128)(2,1)} %get-tuple-element.6, bf16[224,3584]{1,0:T(8,128)(2,1)} %copy-done.1, bf16[224,3584]{1,0:T(8,128)(2,1)S(1)} %get-tuple-element.10), kind=kOutput, calls=%fused_computation | convolution fusion | flops 6671056896 | bytes 33947648 | tf_op jit(solution)/shard_map/dot_general | solution.py:47
  232.9 1.4 reduce_sum.12
  234.3 1.4 fusion.12
  235.8 0.9 copy.12
  236.6 1.2 concatenate.24
  237.8 0.7 constant_dynamic-slice_fusion
  (17 shorter events, 0.4 us)
Async XLA Ops:
  7.2 166.8 %all-reduce.4.cloned.1.call-start = ((), (), s32[]{:S(2)}) async-start(), calls=%async_computation | async-start | bytes 6422528 | tf_op jit(solution)/shard_map/psum | solution.py:35
  30.3 21.6 %copy-start.4 = (bf16[28,2048]{1,0:T(8,128)(2,1)S(1)}, bf16[28,2048]{1,0:T(8,128)(2,1)}, u32[]{:S(2)}) copy-start(bf16[28,2048]{1,0:T(8,128)(2,1)} %param.5) | copy-start | bytes 344068
  70.4 14.8 %copy-start.2 = (bf16[224,2048]{1,0:T(8,128)(2,1)}, bf16[224,2048]{1,0:T(8,128)(2,1)S(1)}, u32[]{:S(2)}) copy-start(bf16[224,2048]{1,0:T(8,128)(2,1)S(1)} %reshape.26) | copy-start | bytes 2752516
  70.4 15.8 %copy-start.5 = (u32[32]{0:T(128)S(1)}, u32[32]{0:T(128)}, u32[]{:S(2)}) copy-start(u32[32]{0:T(128)} %constant.8) | copy-start | bytes 388
  109.1 67.6 %copy-start = (bf16[224,3584]{1,0:T(8,128)(2,1)S(1)}, bf16[224,3584]{1,0:T(8,128)(2,1)}, u32[]{:S(2)}) copy-start(bf16[224,3584]{1,0:T(8,128)(2,1)} %param.6) | copy-start | bytes 4816900
  178.2 1.2 copy-start.1
  179.4 39.3 %copy-start.3 = (bf16[224,2048]{1,0:T(8,128)(2,1)S(1)}, bf16[224,2048]{1,0:T(8,128)(2,1)}, u32[]{:S(2)}) copy-start(bf16[224,2048]{1,0:T(8,128)(2,1)} %copy-done.2) | copy-start | bytes 2752516
  216.7 19.9 %collective-permute-start = (bf16[28,2048]{1,0:T(8,128)(2,1)}, bf16[28,2048]{1,0:T(8,128)(2,1)}, u32[]{:S(2)}, u32[]{:S(2)}) collective-permute-start(bf16[28,2048]{1,0:T(8,128)(2,1)} %slice.38), channel_id=1, source_target_pairs={{0,2},{2,4},{4,6},{6,8},{8,10},{10,12},{12,14},{1,3},{3,5},{5,7},{... | collective-permute-start | bytes 344072
Sparse Core Ops, SparseCore 0:
  85.3 88.6 all-reduce.3
where the time goes:
time: 246 us; the launch traced here: 245 us
  waiting for transfers between devices  65 us (26%)
  local copies, waits for them, and re-layouts  51.3 us (21%)
  matrix products  43.2 us (18%)
  blocking collectives  40.8 us (17%)
  other arithmetic  28.4 us (12%)
  between operations  14.8 us (6%)
    psum x1, waiting for transfers between devices, on_device(): lax.psum(jnp.dot(gathered, joined, preferred_element_type=jnp.float32).as...  65 us
    unnamed x1, blocking collectives  22.4 us
    squeeze x1, local copies, waits for them, and re-layouts, on_device(): codes[0]  21.6 us
    squeeze x1, local copies, waits for them, and re-layouts, dequantize(): return (jnp.concatenate((weight[0], weight[1]), axis=1), factor)  21.6 us
    convert_element_type x1, other arithmetic, dequantize(): weight = values.reshape(codes.shape).astype(jnp.bfloat16)  20.5 us
    all_gather x1, blocking collectives, on_device(): gathered = lax.all_gather(tokens, 'blk', axis=0, tiled=True)  18.3 us
    dot_general x1, matrix products, on_device(): jnp.dot(gathered, joined, preferred_element_type=jnp.float32)  14.7 us
    dot_general x1, matrix products, on_device(): lax.dot_general(gathered, grads, (((0,), (0,)), ((), ())), preferred_elem...  14.2 us
  transfers between devices with their start and end apart: 2, of which 1 were waited for; matrix products, arithmetic and copies ran while one was open for 17% of the time, Pallas kernels for 0%

commit v1 on v0

--- a/solution.py
+++ b/solution.py
@@ -2,6 +2,16 @@
 import jax.numpy as jnp
 from jax import lax
 from jax.sharding import PartitionSpec as P
+
+
+def around_the_ring(x, name, dim):
+    count = lax.axis_size(name)
+    held, pieces = (x, [x])
+    for _ in range(count - 1):
+        held = lax.ppermute(held, name, [(i, (i + 1) % count) for i in range(count)])
+        pieces.insert(0, held)
+    line = jnp.concatenate(pieces, axis=dim)
+    return jnp.roll(line, (lax.axis_index(name) + 1) * x.shape[dim], axis=dim)
 
 
 def dequantize(codes, scales, pattern):
@@ -30,7 +40,7 @@
     cols_tile, rows_tile = pattern.shape
     block = codes.shape[1] // rows_tile
     slice_f = codes.shape[2]
-    gathered = lax.all_gather(tokens, "blk", axis=0, tiled=True)
+    gathered = around_the_ring(tokens, "blk", 0)
     joined, factor = dequantize(codes, scales, pattern)
     hidden = lax.psum(
         jnp.dot(gathered, joined, preferred_element_type=jnp.float32).astype(jnp.bfloat16), "width"

time: 246 us -> 257 us (1.045)
  waiting for transfers between devices: 65 us -> 96.1 us
  blocking collectives: 40.8 us -> 21.9 us
    ppermute x0 -> x7, waiting for transfers between devices: none -> 30.7 us  [around_the_ring(): lax.ppermute(held, name, [(i, (i + 1) % count) for i in range(count)])]
    all_gather x1 -> x0, blocking collectives: 18.3 us -> none  [on_device(): gathered = lax.all_gather(tokens, 'blk', axis=0, tiled=True)]
    unnamed x19 -> x20, local copies, waits for them, and re-layouts: 5.47 us -> 5.12 us
  transfers between devices with their start and end apart: 2 -> 9, of which waited for: 1 -> 6; matrix products, arithmetic and copies ran while one was open for 17% -> 32% of each run, Pallas kernels for 0% -> 0%
where the time goes in v1:
time: 257 us
  waiting for transfers between devices  96.1 us (37%)
  local copies, waits for them, and re-layouts  51.6 us (20%)
  matrix products  42 us (16%)
  other arithmetic  27.5 us (11%)
  blocking collectives  21.9 us (9%)
  between operations  14.9 us (6%)
    psum x1, waiting for transfers between devices, on_device(): lax.psum(jnp.dot(gathered, joined, preferred_element_type=jnp.float32).as...  65.4 us
    ppermute x7, waiting for transfers between devices, around_the_ring(): lax.ppermute(held, name, [(i, (i + 1) % count) for i in range(count)])  30.7 us
    unnamed x1, blocking collectives  21.9 us
    squeeze x1, local copies, waits for them, and re-layouts, on_device(): codes[0]  21.6 us
    squeeze x1, local copies, waits for them, and re-layouts, dequantize(): return (jnp.concatenate((weight[0], weight[1]), axis=1), factor)  21.4 us
    convert_element_type x1, other arithmetic, dequantize(): weight = values.reshape(codes.shape).astype(jnp.bfloat16)  20.5 us
    dot_general x1, matrix products, on_device(): jnp.dot(gathered, joined, preferred_element_type=jnp.float32)  14.7 us
    dot_general x1, matrix products, on_device(): lax.dot_general(gathered, grads, (((0,), (0,)), ((), ())), preferred_elem...  13.9 us
  transfers between devices with their start and end apart: 9, of which 6 were waited for; matrix products, arithmetic and copies ran while one was open for 32% of the time, Pallas kernels for 0%

profile of v1, /device:TPU:0, one launch (start us, length us, event | category | flops | bytes accessed | tf_op | source)
XLA Modules:
  0.0 256.6 jit_solution(14019820833542995489)
XLA Ops:
  7.7 6.9 %collective-permute-done = bf16[28,2048]{1,0:T(8,128)(2,1)S(1)} collective-permute-done((bf16[28,2048]{1,0:T(8,128)(2,1)}, bf16[28,2048]{1,0:T(8,128)(2,1)S(1)}, u32[]{:S(2)}, u32[]{:S(2)}) %collective-permute-start) | collective-permute-done | bytes 114720 | tf_op jit(solution)/shard_map/ppermute | solution.py:11
  14.6 6.2 %collective-permute-done.1 = bf16[28,2048]{1,0:T(8,128)(2,1)S(1)} collective-permute-done((bf16[28,2048]{1,0:T(8,128)(2,1)S(1)}, bf16[28,2048]{1,0:T(8,128)(2,1)S(1)}, u32[]{:S(2)}, u32[]{:S(2)}) %collective-permute-start.1) | collective-permute-done | bytes 114720 | tf_op jit(solution)/shard_map/ppermute | solution.py:11
  20.8 6.2 %collective-permute-done.2 = bf16[28,2048]{1,0:T(8,128)(2,1)S(1)} collective-permute-done((bf16[28,2048]{1,0:T(8,128)(2,1)S(1)}, bf16[28,2048]{1,0:T(8,128)(2,1)S(1)}, u32[]{:S(2)}, u32[]{:S(2)}) %collective-permute-start.2) | collective-permute-done | bytes 114720 | tf_op jit(solution)/shard_map/ppermute | solution.py:11
  27.0 6.2 %collective-permute-done.3 = bf16[28,2048]{1,0:T(8,128)(2,1)S(1)} collective-permute-done((bf16[28,2048]{1,0:T(8,128)(2,1)S(1)}, bf16[28,2048]{1,0:T(8,128)(2,1)S(1)}, u32[]{:S(2)}, u32[]{:S(2)}) %collective-permute-start.3) | collective-permute-done | bytes 114720 | tf_op jit(solution)/shard_map/ppermute | solution.py:11
  33.2 0.7 convert_bitcast_fusion
  34.2 5.2 %collective-permute-done.4 = bf16[28,2048]{1,0:T(8,128)(2,1)S(1)} collective-permute-done((bf16[28,2048]{1,0:T(8,128)(2,1)S(1)}, bf16[28,2048]{1,0:T(8,128)(2,1)S(1)}, u32[]{:S(2)}, u32[]{:S(2)}) %collective-permute-start.4) | collective-permute-done | bytes 114720 | tf_op jit(solution)/shard_map/ppermute | solution.py:11
  39.4 1.5 copy_multiply_fusion
  41.0 20.5 %fusion.1 = bf16[2,2048,3584]{2,1,0:T(8,128)(2,1)} fusion(bf16[2,2048,3584]{2,1,0:T(8,128)(2,1)} %param.7, f32[2,16,3584]{2,1,0:T(8,128)S(1)} %copy.11), kind=kLoop, calls=%fused_computation.2 | loop fusion | flops 44040192 | bytes 59179008 | tf_op jit(solution)/shard_map/convert_element_type | solution.py:24
  61.5 21.4 %slice_bitcast_fusion.1 = (bf16[2048,3584]{1,0:T(8,128)(2,1)}, bf16[2048,3584]{1,0:T(8,128)(2,1)}) fusion(bf16[2,2048,3584]{2,1,0:T(8,128)(2,1)} %fusion.1), kind=kLoop, calls=%fused_computation.8 | loop fusion | bytes 58720256 | tf_op jit(solution)/shard_map/squeeze | solution.py:25
  82.9 1.8 concatenate.24
  84.7 14.7 %fusion.4 = bf16[224,7168]{1,0:T(8,128)(2,1)} fusion(bf16[2048,3584]{1,0:T(8,128)(2,1)} %get-tuple-element.9, bf16[2048,3584]{1,0:T(8,128)(2,1)} %get-tuple-element.8, bf16[448,2048]{1,0:T(8,128)(2,1)S(1)} %concatenate.24, s32[]{:T(128)S(6)} %select_n.14), kind=kOutput, calls=%fused_computation.11 | convolution fusion | flops 6636994560 | bytes 33488900 | tf_op jit(solution)/shard_map/dot_general | solution.py:46
  99.4 1.1 slice_bitcast_fusion.5
  101.8 21.6 %slice_bitcast_fusion.3 = (bf16[2048,3584]{1,0:T(8,128)(2,1)}, bf16[2048,3584]{1,0:T(8,128)(2,1)}) fusion(bf16[2,2048,3584]{2,1,0:T(8,128)(2,1)} %param.7), kind=kLoop, calls=%fused_computation.10 | loop fusion | bytes 58720256 | tf_op jit(solution)/shard_map/squeeze | solution.py:60
  123.4 65.4 %all-reduce.4.cloned.1.call-done = bf16[224,7168]{1,0:T(8,128)(2,1)} async-done(((bf16[224,7168]{1,0:T(8,128)(2,1)}), bf16[224,7168]{1,0:T(8,128)(2,1)}) %all-reduce.4.cloned.1.call-update) | async-done | bytes 3211280 | tf_op jit(solution)/shard_map/psum | solution.py:45
  188.8 2.8 %convert_element_type.43 = f32[224,7168]{1,0:T(8,128)S(1)} convert(bf16[224,7168]{1,0:T(8,128)(2,1)} %all-reduce.4.cloned.1.call-done) | non-fusion elementwise | flops 1605632 | bytes 9633792 | tf_op jit(solution)/shard_map/convert_element_type | solution.py:47
  191.6 1.5 fusion.7
  193.2 1.1 copy-done.1
  194.8 13.4 %fusion.10 = bf16[224,2048]{1,0:T(8,128)(2,1)S(1)} fusion(bf16[2048,3584]{1,0:T(8,128)(2,1)} %get-tuple-element.9, bf16[2048,3584]{1,0:T(8,128)(2,1)} %get-tuple-element.8, bf16[224,3584]{1,0:T(8,128)(2,1)S(1)} %get-tuple-element.11, bf16[224,3584]{1,0:T(8,128)(2,1)S(1)} %get-tuple-element.10), kind=kOutput, calls=%fused_computation.21 | convolution fusion | flops 6642270208 | bytes 33488896 | tf_op jit(solution)/shard_map/dot_general | solution.py:50
  208.2 21.9 %fusion = bf16[32,2048]{1,0:T(8,128)(2,1)S(1)} fusion(bf16[224,2048]{1,0:T(8,128)(2,1)S(1)} %fusion.10), kind=kCustom, calls=%all-reduce-scatter | all-reduce-scatter fusion | flops 524289 | bytes 1049088
  230.2 1.9 collective-permute-start.7
  232.1 13.9 %bitcast_reduce_fusion = f32[16,7168]{1,0:T(8,128)S(1)} fusion(bf16[2048,3584]{1,0:T(8,128)(2,1)} %get-tuple-element.7, bf16[2048,3584]{1,0:T(8,128)(2,1)} %get-tuple-element.6, bf16[224,3584]{1,0:T(8,128)(2,1)} %copy-done.2, bf16[224,3584]{1,0:T(8,128)(2,1)} %copy-done.1, bf16[448,2048]{1,0:T(8,128)(2,1)S(1)} %concatenate.24, s32[]{:T(128)S(6)} %select_n.14), kind=kOutput, calls=%fused_computation | convolution fusion | flops 6671056896 | bytes 33947652 | tf_op jit(solution)/shard_map/dot_general | solution.py:57
  247.0 0.9 copy.12
  247.8 1.2 concatenate.31
  249.0 0.7 constant_dynamic-slice_fusion
  (32 shorter events, 3.0 us)
Async XLA Ops:
  7.2 181.7 %all-reduce.4.cloned.1.call-start = ((), (), s32[]{:S(2)}) async-start(), calls=%async_computation | async-start | bytes 6422528 | tf_op jit(solution)/shard_map/psum | solution.py:45
  7.2 7.4 %collective-permute-start = (bf16[28,2048]{1,0:T(8,128)(2,1)}, bf16[28,2048]{1,0:T(8,128)(2,1)S(1)}, u32[]{:S(2)}, u32[]{:S(2)}) collective-permute-start(bf16[28,2048]{1,0:T(8,128)(2,1)} %param.5), channel_id=1, source_target_pairs={{0,2},{2,4},{4,6},{6,8},{8,10},{10,12},{12,14},{14,0},{1,3},{3,5},... | collective-permute-start | bytes 344072 | tf_op jit(solution)/shard_map/ppermute | solution.py:11
  14.6 6.2 %collective-permute-start.1 = (bf16[28,2048]{1,0:T(8,128)(2,1)S(1)}, bf16[28,2048]{1,0:T(8,128)(2,1)S(1)}, u32[]{:S(2)}, u32[]{:S(2)}) collective-permute-start(bf16[28,2048]{1,0:T(8,128)(2,1)S(1)} %collective-permute-done), channel_id=1, source_target_pairs={{0,2},{2,4},{4,6},{6,8},{8,10},{10,12},{12,14},{14,0},{1,3},{3,5},... | collective-permute-start | bytes 344072 | tf_op jit(solution)/shard_map/ppermute | solution.py:11
  20.8 6.2 %collective-permute-start.2 = (bf16[28,2048]{1,0:T(8,128)(2,1)S(1)}, bf16[28,2048]{1,0:T(8,128)(2,1)S(1)}, u32[]{:S(2)}, u32[]{:S(2)}) collective-permute-start(bf16[28,2048]{1,0:T(8,128)(2,1)S(1)} %collective-permute-done.1), channel_id=1, source_target_pairs={{0,2},{2,4},{4,6},{6,8},{8,10},{10,12},{12,14},{14,0},{1,3},{3,5},... | collective-permute-start | bytes 344072 | tf_op jit(solution)/shard_map/ppermute | solution.py:11
  27.0 6.2 %collective-permute-start.3 = (bf16[28,2048]{1,0:T(8,128)(2,1)S(1)}, bf16[28,2048]{1,0:T(8,128)(2,1)S(1)}, u32[]{:S(2)}, u32[]{:S(2)}) collective-permute-start(bf16[28,2048]{1,0:T(8,128)(2,1)S(1)} %collective-permute-done.2), channel_id=1, source_target_pairs={{0,2},{2,4},{4,6},{6,8},{8,10},{10,12},{12,14},{14,0},{1,3},{3,5},... | collective-permute-start | bytes 344072 | tf_op jit(solution)/shard_map/ppermute | solution.py:11
  33.2 6.2 %collective-permute-start.4 = (bf16[28,2048]{1,0:T(8,128)(2,1)S(1)}, bf16[28,2048]{1,0:T(8,128)(2,1)S(1)}, u32[]{:S(2)}, u32[]{:S(2)}) collective-permute-start(bf16[28,2048]{1,0:T(8,128)(2,1)S(1)} %collective-permute-done.3), channel_id=1, source_target_pairs={{0,2},{2,4},{4,6},{6,8},{8,10},{10,12},{12,14},{14,0},{1,3},{3,5},... | collective-permute-start | bytes 344072 | tf_op jit(solution)/shard_map/ppermute | solution.py:11
  39.4 22.1 %collective-permute-start.5 = (bf16[28,2048]{1,0:T(8,128)(2,1)S(1)}, bf16[28,2048]{1,0:T(8,128)(2,1)S(1)}, u32[]{:S(2)}, u32[]{:S(2)}) collective-permute-start(bf16[28,2048]{1,0:T(8,128)(2,1)S(1)} %collective-permute-done.4), channel_id=1, source_target_pairs={{0,2},{2,4},{4,6},{6,8},{8,10},{10,12},{12,14},{14,0},{1,3},{3,5},... | collective-permute-start | bytes 344072 | tf_op jit(solution)/shard_map/ppermute | solution.py:11
  61.4 21.4 %copy-start.5 = (bf16[28,2048]{1,0:T(8,128)(2,1)S(1)}, bf16[28,2048]{1,0:T(8,128)(2,1)}, u32[]{:S(2)}) copy-start(bf16[28,2048]{1,0:T(8,128)(2,1)} %param.5) | copy-start | bytes 344068
  61.5 21.4 %collective-permute-start.6 = (bf16[28,2048]{1,0:T(8,128)(2,1)S(1)}, bf16[28,2048]{1,0:T(8,128)(2,1)S(1)}, u32[]{:S(2)}, u32[]{:S(2)}) collective-permute-start(bf16[28,2048]{1,0:T(8,128)(2,1)S(1)} %collective-permute-done.5), channel_id=1, source_target_pairs={{0,2},{2,4},{4,6},{6,8},{8,10},{10,12},{12,14},{14,0},{1,3},{3,5},... | collective-permute-start | bytes 344072 | tf_op jit(solution)/shard_map/ppermute | solution.py:11
  84.7 15.8 %copy-start.6 = (u32[32]{0:T(128)S(1)}, u32[32]{0:T(128)}, u32[]{:S(2)}) copy-start(u32[32]{0:T(128)} %constant.37) | copy-start | bytes 388
  188.8 2.8 %copy-start = (bf16[224,3584]{1,0:T(8,128)(2,1)S(1)}, bf16[224,3584]{1,0:T(8,128)(2,1)}, u32[]{:S(2)}) copy-start(bf16[224,3584]{1,0:T(8,128)(2,1)} %param.6) | copy-start | bytes 4816900
  193.1 1.1 copy-start.1
  193.2 1.6 copy-start.2
  230.2 17.7 %collective-permute-start.7 = (bf16[28,2048]{1,0:T(8,128)(2,1)S(1)}, bf16[28,2048]{1,0:T(8,128)(2,1)}, u32[]{:S(2)}, u32[]{:S(2)}) collective-permute-start(bf16[28,2048]{1,0:T(8,128)(2,1)S(1)} %slice.38), channel_id=1, source_target_pairs={{0,2},{2,4},{4,6},{6,8},{8,10},{10,12},{12,14},{1,3},{3,5},{5,7},{... | collective-permute-start | bytes 344072
  232.1 14.3 %copy-start.3 = (f32[16,1,3584]{2,1,0:T(1,128)S(1)}, f32[16,1,3584]{2,1,0:T(1,128)}, u32[]{:S(2)}) copy-start(f32[16,1,3584]{2,1,0:T(1,128)} %get-tuple-element.12) | copy-start | bytes 688132
  232.1 14.4 %copy-start.4 = (f32[16,1,3584]{2,1,0:T(1,128)S(1)}, f32[16,1,3584]{2,1,0:T(1,128)}, u32[]{:S(2)}) copy-start(f32[16,1,3584]{2,1,0:T(1,128)} %get-tuple-element.13) | copy-start | bytes 688132
Sparse Core Ops, SparseCore 0:
  99.5 89.2 all-reduce.3
